TPU v7x, 512 devices: a whole 4x4x16 slice. The times are simulated.
512 devices in a mesh: rep: 8 (over x, core), feat: 64 (over z, y).
Axes of the slice: x: 4, y: 4, z: 16, core: 2. Of those that a mesh axis runs over, the one named last changes fastest.
Arguments:
- features: bfloat16 [8, 768, 32768], P('rep', 'feat'), may hold values from -6 to 6
- w_self: bfloat16 [768, 256], P('feat'), may hold values from -0.21875 to 0.21875
- w_neighbor: bfloat16 [768, 256], P('feat'), may hold values from -0.4375 to 0.4375
- tile_list: int32 [192, 16], P('rep'), may hold values from 0 to 255
- nbr_slot: int32 [24576, 10], P('rep'), may hold values from 0 to 2047
- seed_ids: int32 [24576], P('rep'), may hold values from 0 to 32767
- d_hidden: bfloat16 [24576, 256], P(('rep', 'feat')), may hold values from -6 to 6
Outputs:
- hidden: bfloat16 [24576, 256], P(('rep', 'feat'))
- grad_self: float32 [768, 256], P('feat')
- grad_neighbor: float32 [768, 256], P('feat')
Inputs may be any that keep to these rules, and one draw needn't show every extreme that they name: `tile_list`: source tile ids of the minibatch. `nbr_slot`: a position in the concatenation of the tile's 16 listed tiles.
All inputs are finite; a program needn't handle non-finite values.
Results may differ from a plain program's by a relative error of at most 0.014.
Values may be sent and summed in bfloat16 or wider, within the bound.
A program may use at most 64 MiB of HBM per device.

v0:
```python
import jax
import jax.numpy as jnp
from jax import lax
from jax.sharding import PartitionSpec as P


def contract_rows(left, right):
    return lax.dot_general(
        left, right, (((0,), (0,)), ((), ())), preferred_element_type=jnp.float32
    )


def local(features, w_self, w_neighbor, tile_list, nbr_slot, seed_ids, d_hidden):
    local_feat = features[0]
    width_here = local_feat.shape[0]
    tile_count = tile_list.shape[0]
    fanout = nbr_slot.shape[1]
    tile_rows = nbr_slot.shape[0] // tile_count
    self_feat = jnp.take(local_feat, seed_ids, axis=1)
    feat_tiles = local_feat.reshape(width_here, -1, tile_rows)

    def tile_mean(tile_pair):
        listed, slots = tile_pair
        picked = jnp.take(feat_tiles, listed, axis=1).reshape(width_here, -1)
        slot_range = jnp.arange(picked.shape[1], dtype=jnp.int32)
        counts = jnp.sum((slots[:, :, None] == slot_range[None, None, :]).astype(jnp.int32), axis=1)
        return jnp.einsum(
            "fs,rs->fr", picked, counts.astype(jnp.bfloat16), preferred_element_type=jnp.float32
        )

    means = lax.map(tile_mean, (tile_list, nbr_slot.reshape(tile_count, tile_rows, fanout)))
    neighbor_mean = (
        jnp.transpose(means, (1, 0, 2)).reshape(width_here, -1) * (1.0 / fanout)
    ).astype(jnp.bfloat16)
    own_part = self_feat
    mean_part = neighbor_mean
    pre = lax.psum_scatter(
        contract_rows(own_part, w_self) + contract_rows(mean_part, w_neighbor),
        "feat",
        scatter_dimension=0,
        tiled=True,
    )
    hidden = jax.nn.silu(pre).astype(jnp.bfloat16)
    sigma = jax.nn.sigmoid(pre)
    d_pre = (d_hidden.astype(jnp.float32) * sigma * (1.0 + pre * (1.0 - sigma))).astype(
        jnp.bfloat16
    )
    piece = lax.all_gather(d_pre, "feat", axis=0, tiled=True)
    own_part = self_feat
    mean_part = neighbor_mean
    grad_own = jnp.dot(own_part, piece, preferred_element_type=jnp.float32)
    grad_mean = jnp.dot(mean_part, piece, preferred_element_type=jnp.float32)
    grad_self, grad_neighbor = lax.psum((grad_own, grad_mean), "rep")
    return (hidden, grad_self, grad_neighbor)


def solution(mesh):
    placed = (
        P("rep", "feat", None),
        P("feat", None),
        P("feat", None),
        P("rep", None),
        P("rep", None),
        P("rep"),
        P(("rep", "feat"), None),
    )
    return jax.shard_map(
        local,
        mesh=mesh,
        in_specs=placed,
        out_specs=(P(("rep", "feat"), None), P("feat", None), P("feat", None)),
        check_vma=False,
    )
```

profile of v0, /device:TPU:1, one launch (start us, length us, event | category | flops | bytes accessed | tf_op | source)
XLA Modules:
  0.0 970.8 jit_solution(8014443438271453961)
XLA Ops:
  8.7 7.4 copy.24
  17.1 60.3 %while.10 = (s32[]{:T(128)}, f32[24,12,128]{2,1,0:T(8,128)S(1)}, s32[24,16]{1,0:T(8,128)S(1)}, bf16[12,256,128]{2,0,1:T(8,128)(2,1)S(1)}, s32[24,128,10]{1,0,2:T(8,128)S(1)}, /*index=5*/s32[]{:T(128)}, bf16[]{:T(256)}) while((s32[]{:T(128)}, f32[24,12,128]{2,1,0:T(8,128)S(1)}, s32[24,16]{1,0:T(8,128)S(1)}, ...), condition=%wide.region_2.3_spmd, body=%wide.region_0.0_spmd.sunk | while | flops 14181522 | bytes 2647487 | solution.py:31
  17.9 1.5 convert_reduce_fusion.2
  20.4 1.5 convert_reduce_fusion.2
  33.0 1.5 convert_reduce_fusion.2
  35.5 1.5 convert_reduce_fusion.2
  38.0 1.5 convert_reduce_fusion.2
  40.5 1.5 convert_reduce_fusion.2
  43.0 1.5 convert_reduce_fusion.2
  48.0 1.5 convert_reduce_fusion.2
  50.5 1.5 convert_reduce_fusion.2
  53.1 1.5 convert_reduce_fusion.2
  63.1 1.5 convert_reduce_fusion.2
  65.6 1.5 convert_reduce_fusion.2
  68.1 1.5 convert_reduce_fusion.2
  70.6 1.5 convert_reduce_fusion.2
  73.1 1.5 convert_reduce_fusion.2
  77.5 12.8 %gather_fusion.1 = bf16[3072,12]{1,0:T(8,128)(2,1)S(1)} fusion(bf16[12,32768]{0,1:T(8,128)(2,1)} %bitcast.59, s32[3072]{0:T(1024)S(1)} %fusion.10), kind=kCustom, calls=%fused_computation.1 | custom fusion | bytes 159744 | tf_op jit(solution)/shard_map/jit(_take)/gather | solution.py:19
  91.4 2.3 convolution_add_fusion
  93.8 692.5 %reduce-scatter.2.cloned.1.call-done = f32[48,256]{1,0:T(8,128)} async-done(((f32[3072,256]{1,0:T(8,128)}), f32[48,256]{1,0:T(8,128)}) %reduce-scatter.2.cloned.1.call-update) | async-done | bytes 49168 | tf_op jit(solution)/shard_map/reduce_scatter | solution.py:37
  787.7 140.9 %all-gather.2.cloned.1.call-done = bf16[3072,256]{1,0:T(8,128)(2,1)} async-done(((bf16[48,256]{1,0:T(8,128)(2,1)}), bf16[3072,256]{1,0:T(8,128)(2,1)}) %all-gather.2.cloned.1.call-update) | async-done | bytes 1572880 | tf_op jit(solution)/shard_map/all_gather | solution.py:48
  928.6 3.0 fusion.8
  931.6 1.7 fusion.13
  933.3 30.7 %all-reduce = (f32[12,256]{1,0:T(8,128)}, f32[12,256]{1,0:T(8,128)}) all-reduce(f32[12,256]{1,0:T(8,128)S(1)} %fusion.8, f32[12,256]{1,0:T(8,128)S(1)} %fusion.13), channel_id=1, replica_groups=mesh['rep'=8,'feat'=64] {'rep'}, use_global_device_ids=true, to_apply=%region_4.5 | all-reduce | flops 6144 | bytes 49152 | tf_op jit(solution)/shard_map/psum | solution.py:53
  (304 shorter events, 42.0 us)
Async XLA Ops:
  7.2 83.1 %copy-start = (bf16[12,256]{1,0:T(8,128)(2,1)S(1)}, bf16[12,256]{1,0:T(8,128)(2,1)}, u32[]{:S(2)}) copy-start(bf16[12,256]{1,0:T(8,128)(2,1)} %param.10) | copy-start | bytes 18436
  7.2 779.0 %reduce-scatter.2.cloned.1.call-start = ((), (), s32[]{:S(2)}) async-start(), calls=%async_computation.1 | async-start | bytes 3194880 | tf_op jit(solution)/shard_map/reduce_scatter | solution.py:37
  8.7 7.4 copy-start.1
  16.0 0.9 copy-start.2
  16.0 1.0 copy-start.5
  77.4 14.1 %copy-start.4 = (bf16[12,256]{1,0:T(8,128)(2,1)S(1)}, bf16[12,256]{1,0:T(8,128)(2,1)}, u32[]{:S(2)}) copy-start(bf16[12,256]{1,0:T(8,128)(2,1)} %param.11) | copy-start | bytes 18436
  93.7 692.5 %copy-start.3 = (bf16[48,256]{1,0:T(8,128)(2,1)S(1)}, bf16[48,256]{1,0:T(8,128)(2,1)}, u32[]{:S(2)}) copy-start(bf16[48,256]{1,0:T(8,128)(2,1)} %param.15) | copy-start | bytes 73732
  93.7 834.9 %all-gather.2.cloned.1.call-start = ((), (), s32[]{:S(2)}) async-start(), calls=%async_computation.2 | async-start | bytes 1597440 | tf_op jit(solution)/shard_map/all_gather | solution.py:48
Sparse Core Ops, SparseCore 0:
  93.8 692.3 reduce-scatter.1
  789.2 139.4 all-gather.1
where the time goes:
time: 972 us; the launch traced here: 971 us
  waiting for transfers between devices  833 us (86%)
  other arithmetic  38.9 us (4%)
  local copies, waits for them, and re-layouts  38.1 us (4%)
  blocking collectives  30.7 us (3%)
  between operations  14.2 us (1%)
  matrix products  14 us (1%)
    reduce_scatter x1, waiting for transfers between devices, local(): lax.psum_scatter(contract_rows(own_part, w_self) + contract_rows(mean_par...  692 us
    all_gather x1, waiting for transfers between devices, local(): piece = lax.all_gather(d_pre, 'feat', axis=0, tiled=True)  141 us
    reduce_sum x24, other arithmetic, tile_mean(): jnp.sum((slots[:, :, None] == slot_range[None, None, :]).astype(jnp.int32...  35.1 us
    psum x1, blocking collectives, local(): grad_self, grad_neighbor = lax.psum((grad_own, grad_mean), 'rep')  30.7 us
  transfers between devices with their start and end apart: 2, of which 2 were waited for; matrix products, arithmetic and copies ran while one was open for 0% of the time, Pallas kernels for 0%

commit v1 on v0

v1 whole, which is shorter than its diff:
```python
import jax
import jax.numpy as jnp
from jax import lax
from jax.experimental import pallas as pl
from jax.experimental.pallas import tpu as pltpu
from jax.sharding import PartitionSpec as P

MESH = pl.DeviceIdType.MESH
F32, BF16 = jnp.float32, jnp.bfloat16
NZ, NY, NR = 16, 4, 8
TILE, TB, FAN, LISTED, NS = 128, 24, 10, 16, 256
WIDTH = 12
ROWS = 2 * WIDTH
OWN = 48
H = 256


def lane_pick(values, lanes):
    return jnp.take_along_axis(values, lanes, axis=1, mode="promise_in_bounds")


def select_tree(level, bits):
    for bit in bits:
        level = [jnp.where(bit, level[i + 1], level[i]) for i in range(0, len(level), 2)]
    return level[0]


def neighbor_sums(tiles_ref, x_ref, slot_ref, t):
    low, high = [], []
    for k in range(LISTED):
        at = pl.multiple_of(tiles_ref[t, k] * TILE, TILE)
        block = x_ref[:, pl.ds(at, TILE)].astype(F32)
        low.append(block[:8])
        high.append(block[8:])
    pairs = [jnp.concatenate(high[k:k + 2], axis=0) for k in range(0, LISTED, 2)]
    upper = lax.broadcasted_iota(jnp.int32, (8, TILE), 0) >= 4
    total_low = jnp.zeros((8, TILE), F32)
    total_pair = jnp.zeros((8, TILE), F32)
    for j in range(FAN):
        slot = jnp.broadcast_to(slot_ref[t, j:j + 1, :], (8, TILE))
        lane = slot & (TILE - 1)
        bits = [(slot & (TILE << b)) != 0 for b in range(4)]
        total_low += select_tree([lane_pick(v, lane) for v in low], bits)
        picked = select_tree([lane_pick(v, lane) for v in pairs], bits[1:])
        total_pair += jnp.where(bits[0] == upper, picked, 0.0)
    return total_low, total_pair[:4] + total_pair[4:]


def gather_kernel(tiles_ref, x_ref, slot_ref, seed_ref, g_ref, wide, turned, rows):
    def fill(k, _):
        block = x_ref[:, pl.ds(pl.multiple_of(k * TILE, TILE), TILE)]
        wide[pl.ds(pl.multiple_of(k * 16, 16), WIDTH)] = block.astype(F32)
        return 0

    lax.fori_loop(0, NS, fill, 0, unroll=8)
    for f in range(WIDTH):
        turned[f] = wide[pl.ds(f, NS, stride=16)].T.astype(BF16)

    def three_tiles(u, _):
        span = 3 * TILE
        seed = jnp.concatenate([seed_ref[3 * u + i] for i in range(3)], axis=1)
        hot = (lax.broadcasted_iota(jnp.int32, (NS, span), 0) == (seed >> 7)).astype(F32).astype(BF16)
        mask = lax.broadcasted_iota(jnp.int32, (TILE, span), 0) == (seed & (TILE - 1))
        for f in range(WIDTH):
            columns = jnp.dot(turned[f], hot, preferred_element_type=F32)
            row = jnp.sum(jnp.where(mask, columns, 0.0), axis=0, keepdims=True)
            for i in range(3):
                rows[i, f:f + 1] = row[:, i * TILE:(i + 1) * TILE]
        for i in range(3):
            low, high = neighbor_sums(tiles_ref, x_ref, slot_ref, 3 * u + i)
            rows[i, WIDTH:16] = high * (1.0 / FAN)
            rows[i, 16:ROWS] = low * (1.0 / FAN)
        first, middle, last = rows[0], rows[1], rows[2]
        front = lax.broadcasted_iota(jnp.int32, (ROWS, TILE), 1) < TILE // 2
        middle_turned = pltpu.roll(middle, TILE // 2, 1)
        last_turned = pltpu.roll(last, TILE // 2, 1)
        g_ref[2 * u] = jnp.concatenate([first, jnp.where(front, middle, 0.0)], axis=0).astype(BF16)
        g_ref[2 * u + 1] = jnp.concatenate(
            [jnp.where(front, middle_turned, last_turned), jnp.where(front, last_turned, 0.0)], axis=0
        ).astype(BF16)
        return 0

    lax.fori_loop(0, TB // 3, three_tiles, 0)


def gather(features, tile_list, nbr_slot, seed_ids):
    slots = jnp.transpose(nbr_slot.reshape(TB, TILE, FAN), (0, 2, 1))
    vmem = pl.BlockSpec(memory_space=pltpu.VMEM)
    return pl.pallas_call(
        gather_kernel,
        out_shape=jax.ShapeDtypeStruct((NZ, 2 * ROWS, TILE), BF16),
        in_specs=[pl.BlockSpec(memory_space=pltpu.SMEM), vmem, vmem, vmem],
        out_specs=vmem,
        scratch_shapes=[
            pltpu.VMEM((NS * 16, TILE), F32),
            pltpu.VMEM((WIDTH, TILE, NS), BF16),
            pltpu.VMEM((3, ROWS, TILE), F32),
        ],
        compiler_params=pltpu.CompilerParams(vmem_limit_bytes=32 * 2**20),
        name="gather",
    )(tile_list, features, slots, seed_ids.reshape(TB, 1, TILE))


def exchange_kernel(
    g_ref, ws_ref, wn_ref, dh_ref, hid_ref, gs_ref, gn_ref,
    xb, wb, pf, ps, pr, db, qf, qs, qr, es, er,
    x_out, x_in, w_out, w_in, p_out, p_in, d_out, d_in, q_out, q_in, e_out, e_in,
):
    rep = lax.axis_index("rep")
    feat = lax.axis_index("feat")
    z, y = feat // NY, feat % NY

    def along_z(o):
        return rep, lax.rem(z + o, NZ) * NY + y

    def along_y(o):
        return rep, z * NY + lax.rem(y + o, NY)

    def along_rep(o):
        return lax.rem(rep + o, NR), feat

    barrier = pltpu.get_barrier_semaphore()

    def greet(way):
        def step(o, _):
            pl.semaphore_signal(barrier, inc=1, device_id=way(o), device_id_type=MESH)
            return 0
        return step

    lax.fori_loop(1, NZ, greet(along_z), 0)
    lax.fori_loop(1, NY, greet(along_y), 0)
    lax.fori_loop(1, NR, greet(along_rep), 0)

    mean_weight = wn_ref[...].astype(F32)
    wb[z] = jnp.concatenate(
        [ws_ref[...].astype(F32), mean_weight[8:], mean_weight[:8], jnp.zeros((8, H), F32)], axis=0
    ).astype(BF16)
    xb[z] = g_ref[z]

    pl.semaphore_wait(barrier, NZ + NY + NR - 3)

    def copy(src, dst, out_sem, in_sem, o, target):
        return pltpu.make_async_remote_copy(
            src_ref=src, dst_ref=dst, send_sem=out_sem.at[o], recv_sem=in_sem.at[o],
            device_id=target, device_id_type=MESH,
        )

    def each(count, body):
        def step(o, _):
            body(o)
            return 0
        lax.fori_loop(1, count, step, 0)

    def x_copy(o, slot):
        return copy(g_ref.at[lax.rem(z + o, NZ)], xb.at[slot], x_out, x_in, o, along_z(o))

    def w_copy(o, slot):
        return copy(wb.at[z], wb.at[slot], w_out, w_in, o, along_z(o))

    def p_copy(o, slot):
        return copy(ps.at[lax.rem(y + o, NY)], pr.at[slot], p_out, p_in, o, along_y(o))

    def d_copy(o, slot):
        return copy(db.at[y], db.at[slot], d_out, d_in, o, along_y(o))

    def q_copy(o, slot):
        return copy(qs.at[lax.rem(z + o, NZ)], qr.at[slot], q_out, q_in, o, along_z(o))

    def e_copy(o, slot):
        return copy(es, er.at[slot], e_out, e_in, o, along_rep(o))

    def behind(place, o, count):
        return lax.rem(place + count - o, count)

    each(NZ, lambda o: x_copy(o, z).start())
    each(NZ, lambda o: w_copy(o, z).start())
    each(NZ, lambda o: w_copy(o, behind(z, o, NZ)).wait_recv())
    each(NZ, lambda o: x_copy(o, behind(z, o, NZ)).wait_recv())

    wide = xb[...].astype(F32)
    x = jnp.concatenate([wide[:, :ROWS], wide[:, ROWS:]], axis=2).reshape(NZ * ROWS, 2 * TILE).astype(BF16)
    w = wb[...].astype(F32)[:, :ROWS].reshape(NZ * ROWS, H).astype(BF16)
    part = lax.dot_general(x, w, (((0,), (0,)), ((), ())), preferred_element_type=F32)
    for i in range(NY):
        pf[i] = part[i * OWN:(i + 1) * OWN]
        ps[i] = part[i * OWN:(i + 1) * OWN].astype(BF16)
    each(NY, lambda o: p_copy(o, y).start())
    pr[y] = jnp.zeros((OWN, H), BF16)
    each(NY, lambda o: p_copy(o, behind(y, o, NY)).wait_recv())
    pre = pf[y] + jnp.sum(pr[...].astype(F32), axis=0)

    sigma = jax.nn.sigmoid(pre)
    db[y] = (dh_ref[...].astype(F32) * sigma * (1.0 + pre * (1.0 - sigma))).astype(BF16)
    each(NY, lambda o: d_copy(o, y).start())
    hid_ref[...] = (pre * sigma).astype(BF16)
    each(NY, lambda o: d_copy(o, behind(y, o, NY)).wait_recv())

    d_pre = jnp.concatenate(
        [db[...].reshape(NY * OWN, H), jnp.zeros((2 * TILE - NY * OWN, H), BF16)], axis=0
    )
    grad = jnp.dot(x, d_pre, preferred_element_type=F32).reshape(NZ, ROWS, H)
    grad = jnp.concatenate([grad[:, :, :TILE], grad[:, :, TILE:]], axis=1)
    qf[...] = grad
    qs[...] = grad.astype(BF16)
    each(NZ, lambda o: q_copy(o, z).start())
    qr[z] = jnp.zeros((2 * ROWS, TILE), BF16)
    each(NZ, lambda o: q_copy(o, behind(z, o, NZ)).wait_recv())
    mine = qf[z] + jnp.sum(qr[...].astype(F32), axis=0)

    es[...] = mine.astype(BF16)
    each(NR, lambda o: e_copy(o, rep).start())
    er[rep] = mine.astype(BF16)
    each(NR, lambda o: e_copy(o, behind(rep, o, NR)).wait_recv())
    total = jnp.sum(er[...].astype(F32), axis=0)
    total = jnp.concatenate([total[:ROWS], total[ROWS:]], axis=1)
    gs_ref[...] = total[:WIDTH]
    gn_ref[:8] = total[16:]
    gn_ref[8:] = total[WIDTH:16]

    each(NZ, lambda o: x_copy(o, z).wait_send())
    each(NZ, lambda o: w_copy(o, z).wait_send())
    each(NY, lambda o: p_copy(o, y).wait_send())
    each(NY, lambda o: d_copy(o, y).wait_send())
    each(NZ, lambda o: q_copy(o, z).wait_send())
    each(NR, lambda o: e_copy(o, rep).wait_send())


def exchange(gathered, w_self, w_neighbor, d_hidden):
    vmem = pl.BlockSpec(memory_space=pltpu.VMEM)
    dma = pltpu.SemaphoreType.DMA
    return pl.pallas_call(
        exchange_kernel,
        out_shape=(
            jax.ShapeDtypeStruct((OWN, H), BF16),
            jax.ShapeDtypeStruct((WIDTH, H), F32),
            jax.ShapeDtypeStruct((WIDTH, H), F32),
        ),
        in_specs=[vmem] * 4,
        out_specs=(vmem,) * 3,
        scratch_shapes=[
            pltpu.VMEM((NZ, 2 * ROWS, TILE), BF16),
            pltpu.VMEM((NZ, 32, H), BF16),
            pltpu.VMEM((NY, OWN, H), F32),
            pltpu.VMEM((NY, OWN, H), BF16),
            pltpu.VMEM((NY, OWN, H), BF16),
            pltpu.VMEM((NY, OWN, H), BF16),
            pltpu.VMEM((NZ, 2 * ROWS, TILE), F32),
            pltpu.VMEM((NZ, 2 * ROWS, TILE), BF16),
            pltpu.VMEM((NZ, 2 * ROWS, TILE), BF16),
            pltpu.VMEM((2 * ROWS, TILE), BF16),
            pltpu.VMEM((NR, 2 * ROWS, TILE), BF16),
        ]
        + [dma((n,)) for n in (NZ, NZ, NZ, NZ, NY, NY, NY, NY, NZ, NZ, NR, NR)],
        compiler_params=pltpu.CompilerParams(
            collective_id=0, has_side_effects=True, vmem_limit_bytes=32 * 2**20
        ),
        name="exchange",
    )(gathered, w_self, w_neighbor, d_hidden)


def local(features, w_self, w_neighbor, tile_list, nbr_slot, seed_ids, d_hidden):
    gathered = gather(features[0], tile_list, nbr_slot, seed_ids)
    return exchange(gathered, w_self, w_neighbor, d_hidden)


def solution(mesh):
    placed = (
        P("rep", "feat", None),
        P("feat", None),
        P("feat", None),
        P("rep", None),
        P("rep", None),
        P("rep"),
        P(("rep", "feat"), None),
    )
    return jax.shard_map(
        local,
        mesh=mesh,
        in_specs=placed,
        out_specs=(P(("rep", "feat"), None), P("feat", None), P("feat", None)),
        check_vma=False,
    )
```

time: 972 us -> 82.3 us (0.08)
  waiting for transfers between devices: 833 us -> 0 us
  Pallas kernels: 0 us -> 75.8 us
  other arithmetic: 38.9 us -> 0 us
  local copies, waits for them, and re-layouts: 38.1 us -> 5.5 us
  blocking collectives: 30.7 us -> 0 us
  matrix products: 14 us -> 0 us
  between operations: 14.2 us -> 0.68 us
    reduce_scatter x1 -> x0, waiting for transfers between devices: 692 us -> none  [local(): lax.psum_scatter(contract_rows(own_part, w_self) + contract_rows(mean_par...]
    all_gather x1 -> x0, waiting for transfers between devices: 141 us -> none  [local(): piece = lax.all_gather(d_pre, 'feat', axis=0, tiled=True)]
    pallas_call x0 -> x2, Pallas kernels: none -> 75.8 us  [the longest x1 67.5 us: exchange(): pl.pallas_call(exchange_kernel, out_shape=(jax.ShapeDtypeStruct((OWN, H),...]
    reduce_sum x24 -> x0, other arithmetic: 35.1 us -> none  [tile_mean(): jnp.sum((slots[:, :, None] == slot_range[None, None, :]).astype(jnp.int32...]
    psum x1 -> x0, blocking collectives: 30.7 us -> none  [local(): grad_self, grad_neighbor = lax.psum((grad_own, grad_mean), 'rep')]
    gather x49 -> x0, local copies, waits for them, and re-layouts: 26.9 us -> none  [the longest x48 14.2 us: tile_mean(): picked = jnp.take(feat_tiles, listed, axis=1).reshape(width_here, -1)]
    dot_general x28 -> x0, matrix products: 14 us -> none  [the longest x24 5.9 us: tile_mean(): jnp.einsum('fs,rs->fr', picked, counts.astype(jnp.bfloat16), preferred_el...]
  transfers between devices with their start and end apart: 2 -> 0, of which waited for: 2 -> 0; matrix products, arithmetic and copies ran while one was open for 0% -> 0% of each run, Pallas kernels for 0% -> 0%
where the time goes in v1:
time: 82.3 us; the launch traced here: 82 us
  Pallas kernels  75.8 us (92%)
  local copies, waits for them, and re-layouts  5.5 us (7%)
    pallas_call x1, Pallas kernels, exchange(): pl.pallas_call(exchange_kernel, out_shape=(jax.ShapeDtypeStruct((OWN, H),...  67.5 us
    pallas_call x1, Pallas kernels, gather(): pl.pallas_call(gather_kernel, out_shape=jax.ShapeDtypeStruct((NZ, 2 * ROW...  8.34 us
    unnamed x15, local copies, waits for them, and re-layouts  5.45 us

profile of v1, /device:TPU:1, one launch (start us, length us, event | category | flops | bytes accessed | tf_op | source)
XLA Modules:
  0.0 82.0 jit_solution(18055769806037781766)
XLA Ops:
  0.6 0.8 copy.12.tiles_ref
  1.4 1.0 %copy.13 = s32[2,8,24,128]{3,2,1,0:T(8,128)S(1)} copy(s32[2,8,24,128]{3,1,2,0:T(8,128)} %bitcast.15) | data formatting | bytes 393216
  2.4 0.0 copy-start.2
  2.4 0.7 copy-done.2
  3.1 0.0 copy-start
  3.1 1.2 %copy-done = bf16[1,12,32768]{2,1,0:T(8,128)(2,1)S(1)} copy-done((bf16[1,12,32768]{2,1,0:T(8,128)(2,1)S(1)}, bf16[1,12,32768]{2,1,0:T(8,128)(2,1)}, u32[]{:S(2)}) %copy-start) | copy-done | bytes 786456
  4.3 0.0 copy-start.1
  4.3 0.0 copy-start.3
  4.3 0.0 copy-start.4
  4.3 8.3 %gather.1.g_ref = bf16[16,48,128]{2,1,0:T(8,128)(2,1)S(1)} custom-call(s32[24,16]{1,0:T(8,128)S(1)} %copy.12.tiles_ref, bf16[12,32768]{1,0:T(8,128)(2,1)S(1)} %bitcast.11, s32[24,10,128]{2,1,0:T(8,128)S(1)} %bitcast.12, s32[24,1,128]{2,1,0:T(1,128)S(1)} %bitcast.13), custom_call_target="tpu_custom_call" | custom-call | tf_op jit(solution)/shard_map/gather/pallas_call | solution.py:89
  12.7 0.0 copy-done.1
  12.7 0.0 copy-done.3
  12.7 0.0 copy-done.4
  12.7 67.5 %exchange.1 = (bf16[48,256]{1,0:T(8,128)(2,1)S(1)}, f32[12,256]{1,0:T(8,128)S(1)}, f32[12,256]{1,0:T(8,128)S(1)}) custom-call(bf16[16,48,128]{2,1,0:T(8,128)(2,1)S(1)} %gather.1.g_ref, bf16[12,256]{1,0:T(8,128)(2,1)S(1)} %copy-done.3, bf16[12,256]{1,0:T(8,128)(2,1)S(1)} %copy-done.4, bf16[48,256]{1,0:T(8,128)(2,1)S(1)} %copy-done.1), custom_call_target="tpu_custom_call" | custom-call | tf_op jit(solution)/shard_map/exchange/pallas_call | solution.py:231
  80.2 0.6 copy.19
  80.8 0.6 copy.20
  81.4 0.6 copy.21
  (2 shorter events, 0.0 us)
Async XLA Ops:
  2.4 0.7 copy-start.2
  3.1 1.2 %copy-start = (bf16[1,12,32768]{2,1,0:T(8,128)(2,1)S(1)}, bf16[1,12,32768]{2,1,0:T(8,128)(2,1)}, u32[]{:S(2)}) copy-start(bf16[1,12,32768]{2,1,0:T(8,128)(2,1)} %param.7) | copy-start | bytes 2359300
  4.3 8.3 %copy-start.1 = (bf16[48,256]{1,0:T(8,128)(2,1)S(1)}, bf16[48,256]{1,0:T(8,128)(2,1)}, u32[]{:S(2)}) copy-start(bf16[48,256]{1,0:T(8,128)(2,1)} %dh_ref.1) | copy-start | bytes 73732
  4.3 8.3 %copy-start.3 = (bf16[12,256]{1,0:T(8,128)(2,1)S(1)}, bf16[12,256]{1,0:T(8,128)(2,1)}, u32[]{:S(2)}) copy-start(bf16[12,256]{1,0:T(8,128)(2,1)} %ws_ref.1) | copy-start | bytes 18436
  4.3 8.3 %copy-start.4 = (bf16[12,256]{1,0:T(8,128)(2,1)S(1)}, bf16[12,256]{1,0:T(8,128)(2,1)}, u32[]{:S(2)}) copy-start(bf16[12,256]{1,0:T(8,128)(2,1)} %wn_ref.1) | copy-start | bytes 18436

commit v2 on v1

v2 whole, which is shorter than its diff:
```python
import jax
import jax.numpy as jnp
from jax import lax
from jax.experimental import pallas as pl
from jax.experimental.pallas import tpu as pltpu
from jax.sharding import PartitionSpec as P

MESH = pl.DeviceIdType.MESH
F32, BF16 = jnp.float32, jnp.bfloat16
NZ, NY, NR = 16, 4, 8
TILE, TB, FAN, LISTED, NS = 128, 24, 10, 16, 256
WIDTH = 12
ROWS = 2 * WIDTH
OWN = 48
H = 256
CHUNKS = 4
SPREAD = 4


def lane_pick(values, lanes):
    return jnp.take_along_axis(values, lanes, axis=1, mode="promise_in_bounds")


def select_tree(level, bits):
    for bit in bits:
        level = [jnp.where(bit, level[i + 1], level[i]) for i in range(0, len(level), 2)]
    return level[0]


def neighbor_sums(tiles_ref, wide, slot_ref, t):
    low, high = [], []
    for k in range(LISTED):
        block = wide[tiles_ref[k, t]]
        low.append(block[:8])
        high.append(block[8:WIDTH])
    pairs = [jnp.concatenate(high[k:k + 2], axis=0) for k in range(0, LISTED, 2)]
    upper = lax.broadcasted_iota(jnp.int32, (8, TILE), 0) >= 4
    total_low = jnp.zeros((8, TILE), F32)
    total_pair = jnp.zeros((8, TILE), F32)
    targets = pl.ds(pl.multiple_of(t * TILE, TILE), TILE)
    for j in range(FAN):
        slot = jnp.broadcast_to(slot_ref[j:j + 1, targets], (8, TILE))
        lane = slot & (TILE - 1)
        bits = [(slot & (TILE << b)) != 0 for b in range(4)]
        total_low += select_tree([lane_pick(v, lane) for v in low], bits)
        picked = select_tree([lane_pick(v, lane) for v in pairs], bits[1:])
        total_pair += jnp.where(bits[0] == upper, picked, 0.0)
    return total_low, total_pair[:4] + total_pair[4:]


def prepare(x_ref, wide, first_tile, tiles):
    def fill(k, _):
        block = x_ref[:, pl.ds(pl.multiple_of(k * TILE, TILE), TILE)]
        wide[k, :WIDTH] = block.astype(F32)
        return 0

    lax.fori_loop(first_tile, first_tile + tiles, fill, 0, unroll=8)


def gather_blocks(tiles_ref, wide, slot_ref, seed_ref, turned, rows, gb, u):
    span = 3 * TILE
    seed = jnp.concatenate([seed_ref[3 * u + i] for i in range(3)], axis=1)
    hot = (lax.broadcasted_iota(jnp.int32, (NS, span), 0) == (seed >> 7)).astype(F32).astype(BF16)
    mask = lax.broadcasted_iota(jnp.int32, (TILE, span), 0) == (seed & (TILE - 1))
    for f in range(WIDTH):
        columns = jnp.dot(turned[f], hot, preferred_element_type=F32)
        row = jnp.sum(jnp.where(mask, columns, 0.0), axis=0, keepdims=True)
        for i in range(3):
            rows[i, f:f + 1] = row[:, i * TILE:(i + 1) * TILE]
    for i in range(3):
        low, high = neighbor_sums(tiles_ref, wide, slot_ref, 3 * u + i)
        rows[i, WIDTH:16] = high * (1.0 / FAN)
        rows[i, 16:ROWS] = low * (1.0 / FAN)
    first, middle, last = rows[0], rows[1], rows[2]
    front = lax.broadcasted_iota(jnp.int32, (ROWS, TILE), 1) < TILE // 2
    middle_turned = pltpu.roll(middle, TILE // 2, 1)
    last_turned = pltpu.roll(last, TILE // 2, 1)
    gb[2 * u] = jnp.concatenate([first, jnp.where(front, middle, 0.0)], axis=0).astype(BF16)
    gb[2 * u + 1] = jnp.concatenate(
        [jnp.where(front, middle_turned, last_turned), jnp.where(front, last_turned, 0.0)], axis=0
    ).astype(BF16)


def sage_kernel(
    x_hbm, tiles_hbm, slot_hbm, seed_hbm, ws_ref, wn_ref, dh_ref, hid_ref, gs_ref, gn_ref,
    x_ref, tiles_ref, slot_ref, seed_ref, wide, turned, rows, gb,
    xb, wb, pf, ps, pr, db, qf, qs, qr, es, er,
    l_in, x_out, x_in, w_out, w_in, v_out, v_in, p_out, p_in, d_out, d_in, q_out, q_in, e_out, e_in,
):
    rep = lax.axis_index("rep")
    feat = lax.axis_index("feat")
    z, y = feat // NY, feat % NY
    chunk = NS * TILE // CHUNKS

    loads = [
        pltpu.make_async_copy(
            x_hbm.at[:, pl.ds(i * chunk, chunk)], x_ref.at[:, pl.ds(i * chunk, chunk)], l_in.at[i]
        )
        for i in range(CHUNKS)
    ] + [
        pltpu.make_async_copy(tiles_hbm, tiles_ref, l_in.at[CHUNKS]),
        pltpu.make_async_copy(slot_hbm, slot_ref, l_in.at[CHUNKS + 1]),
        pltpu.make_async_copy(seed_hbm, seed_ref, l_in.at[CHUNKS + 2]),
    ]
    for load in loads:
        load.start()

    def along_z(o):
        return rep, lax.rem(z + o, NZ) * NY + y

    def along_y(o):
        return rep, z * NY + lax.rem(y + o, NY)

    def along_rep(o):
        return lax.rem(rep + o, NR), feat

    barrier = pltpu.get_barrier_semaphore()

    def each(count, body):
        def step(o, _):
            body(o)
            return 0
        lax.fori_loop(1, count, step, 0)

    def greet(way):
        return lambda o: pl.semaphore_signal(barrier, inc=1, device_id=way(o), device_id_type=MESH)

    each(NZ, greet(along_z))
    each(NY, greet(along_y))
    each(NR, greet(along_rep))

    def copy(src, dst, out_sem, in_sem, o, target):
        return pltpu.make_async_remote_copy(
            src_ref=src, dst_ref=dst, send_sem=out_sem.at[o], recv_sem=in_sem.at[o],
            device_id=target, device_id_type=MESH,
        )

    def x_copy(o, slot):
        return copy(gb.at[lax.rem(z + o, NZ)], xb.at[slot], x_out, x_in, o, along_z(o))

    def w_copy(o, slot):
        return copy(wb.at[z], wb.at[slot], w_out, w_in, o, along_z(o))

    def v_copy(half, o, slot):
        return pltpu.make_async_remote_copy(
            src_ref=wb.at[slot], dst_ref=wb.at[slot], send_sem=v_out.at[half, o], recv_sem=v_in.at[half, o],
            device_id=along_rep(o), device_id_type=MESH,
        )

    def p_copy(o, slot):
        return copy(ps.at[lax.rem(y + o, NY)], pr.at[slot], p_out, p_in, o, along_y(o))

    def d_copy(o, slot):
        return copy(db.at[y], db.at[slot], d_out, d_in, o, along_y(o))

    def q_copy(o, slot):
        return copy(qs.at[lax.rem(z + o, NZ)], qr.at[slot], q_out, q_in, o, along_z(o))

    def e_copy(o, slot):
        return copy(es, er.at[slot], e_out, e_in, o, along_rep(o))

    def behind(place, o, count):
        return lax.rem(place + count - o, count)

    pl.semaphore_wait(barrier, NZ + NY + NR - 3)

    @pl.when(lax.rem(z, NR) == rep)
    def _():
        mean_weight = wn_ref[...].astype(F32)
        weights = jnp.concatenate([ws_ref[...].astype(F32), mean_weight[8:], mean_weight[:8]], axis=0)
        wb[z] = jnp.concatenate([weights[:, :TILE], weights[:, TILE:]], axis=0).astype(BF16)
        each(NZ, lambda o: w_copy(o, z).start())

    for i in range(CHUNKS):
        loads[i].wait()
        prepare(x_ref, wide, i * (NS // CHUNKS), NS // CHUNKS)
    for f in range(WIDTH):
        turned[f] = wide[:, f].T.astype(BF16)
    for load in loads[CHUNKS:]:
        load.wait()

    def two_blocks(i, _):
        odd = i % 2
        away = odd * (4 - (i + 1) // 2) + (1 - odd) * (4 + i // 2)
        u = (z // 2 + away) % (NZ // 2)
        gather_blocks(tiles_ref, wide, slot_ref, seed_ref, turned, rows, gb, u)
        for e in range(2):
            o = (2 * u + e + NZ - z) % NZ

            @pl.when(o != 0)
            def _():
                x_copy(o, z).start()

            @pl.when(o == 0)
            def _():
                xb[z] = gb[z]

        @pl.when(i == SPREAD)
        def _():
            for half in range(2):
                source = rep + half * NR

                @pl.when(source != z)
                def _():
                    w_copy((z + NZ - source) % NZ, source).wait_recv()

                each(NR, lambda o: v_copy(half, o, source).start())

        return 0

    lax.fori_loop(0, NZ // 2, two_blocks, 0)

    for half in range(2):
        each(NR, lambda o: v_copy(half, o, behind(rep, o, NR) + half * NR).wait_recv())
    w = wb[...].astype(F32)
    w = jnp.concatenate([w[:, :ROWS], w[:, ROWS:]], axis=2).reshape(NZ * ROWS, H).astype(BF16)
    each(NZ, lambda o: x_copy(o, behind(z, o, NZ)).wait_recv())
    x = xb[...].astype(F32)
    x = jnp.concatenate([x[:, :ROWS], x[:, ROWS:]], axis=2).reshape(NZ * ROWS, 2 * TILE).astype(BF16)
    part = lax.dot_general(x, w, (((0,), (0,)), ((), ())), preferred_element_type=F32)
    for i in range(NY):
        pf[i] = part[i * OWN:(i + 1) * OWN]
        ps[i] = part[i * OWN:(i + 1) * OWN].astype(BF16)
    each(NY, lambda o: p_copy(o, y).start())
    pr[y] = jnp.zeros((OWN, H), BF16)
    each(NY, lambda o: p_copy(o, behind(y, o, NY)).wait_recv())
    pre = pf[y] + jnp.sum(pr[...].astype(F32), axis=0)

    sigma = jax.nn.sigmoid(pre)
    db[y] = (dh_ref[...].astype(F32) * sigma * (1.0 + pre * (1.0 - sigma))).astype(BF16)
    each(NY, lambda o: d_copy(o, y).start())
    hid_ref[...] = (pre * sigma).astype(BF16)
    each(NY, lambda o: d_copy(o, behind(y, o, NY)).wait_recv())

    d_pre = jnp.concatenate(
        [db[...].reshape(NY * OWN, H), jnp.zeros((2 * TILE - NY * OWN, H), BF16)], axis=0
    )
    grad = jnp.dot(x, d_pre, preferred_element_type=F32).reshape(NZ, ROWS, H)
    grad = jnp.concatenate([grad[:, :, :TILE], grad[:, :, TILE:]], axis=1)
    qf[...] = grad
    qs[...] = grad.astype(BF16)
    each(NZ, lambda o: q_copy(o, z).start())
    qr[z] = jnp.zeros((2 * ROWS, TILE), BF16)
    each(NZ, lambda o: q_copy(o, behind(z, o, NZ)).wait_recv())
    mine = qf[z] + jnp.sum(qr[...].astype(F32), axis=0)

    es[...] = mine.astype(BF16)
    each(NR, lambda o: e_copy(o, rep).start())
    er[rep] = mine.astype(BF16)
    each(NR, lambda o: e_copy(o, behind(rep, o, NR)).wait_recv())
    total = jnp.sum(er[...].astype(F32), axis=0)
    total = jnp.concatenate([total[:ROWS], total[ROWS:]], axis=1)
    gs_ref[...] = total[:WIDTH]
    gn_ref[:8] = total[16:]
    gn_ref[8:] = total[WIDTH:16]

    @pl.when(lax.rem(z, NR) == rep)
    def _():
        each(NZ, lambda o: w_copy(o, z).wait_send())

    for half in range(2):
        each(NR, lambda o: v_copy(half, o, rep + half * NR).wait_send())
    each(NZ, lambda o: x_copy(o, z).wait_send())
    each(NY, lambda o: p_copy(o, y).wait_send())
    each(NY, lambda o: d_copy(o, y).wait_send())
    each(NZ, lambda o: q_copy(o, z).wait_send())
    each(NR, lambda o: e_copy(o, rep).wait_send())


def local(features, w_self, w_neighbor, tile_list, nbr_slot, seed_ids, d_hidden):
    vmem = pl.BlockSpec(memory_space=pltpu.VMEM)
    anywhere = pl.BlockSpec(memory_space=pl.ANY)
    dma = pltpu.SemaphoreType.DMA
    return pl.pallas_call(
        sage_kernel,
        out_shape=(
            jax.ShapeDtypeStruct((OWN, H), BF16),
            jax.ShapeDtypeStruct((WIDTH, H), F32),
            jax.ShapeDtypeStruct((WIDTH, H), F32),
        ),
        in_specs=[anywhere] * 4 + [vmem] * 3,
        out_specs=(vmem,) * 3,
        scratch_shapes=[
            pltpu.VMEM((WIDTH, NS * TILE), BF16),
            pltpu.SMEM((LISTED, TB), jnp.int32),
            pltpu.VMEM((FAN, TB * TILE), jnp.int32),
            pltpu.VMEM((TB, 1, TILE), jnp.int32),
            pltpu.VMEM((NS, 16, TILE), F32),
            pltpu.VMEM((WIDTH, TILE, NS), BF16),
            pltpu.VMEM((3, ROWS, TILE), F32),
            pltpu.VMEM((NZ, 2 * ROWS, TILE), BF16),
            pltpu.VMEM((NZ, 2 * ROWS, TILE), BF16),
            pltpu.VMEM((NZ, 2 * ROWS, TILE), BF16),
            pltpu.VMEM((NY, OWN, H), F32),
            pltpu.VMEM((NY, OWN, H), BF16),
            pltpu.VMEM((NY, OWN, H), BF16),
            pltpu.VMEM((NY, OWN, H), BF16),
            pltpu.VMEM((NZ, 2 * ROWS, TILE), F32),
            pltpu.VMEM((NZ, 2 * ROWS, TILE), BF16),
            pltpu.VMEM((NZ, 2 * ROWS, TILE), BF16),
            pltpu.VMEM((2 * ROWS, TILE), BF16),
            pltpu.VMEM((NR, 2 * ROWS, TILE), BF16),
        ]
        + [dma((CHUNKS + 3,))]
        + [dma((n,)) for n in (NZ, NZ, NZ, NZ)]
        + [dma((2, NR)), dma((2, NR))]
        + [dma((n,)) for n in (NY, NY, NY, NY, NZ, NZ, NR, NR)],
        compiler_params=pltpu.CompilerParams(
            collective_id=0, has_side_effects=True, vmem_limit_bytes=48 * 2**20
        ),
        name="exchange",
    )(
        features[0], tile_list.T, nbr_slot.T, seed_ids.reshape(TB, 1, TILE), w_self, w_neighbor, d_hidden
    )


def solution(mesh):
    placed = (
        P("rep", "feat", None),
        P("feat", None),
        P("feat", None),
        P("rep", None),
        P("rep", None),
        P("rep"),
        P(("rep", "feat"), None),
    )
    return jax.shard_map(
        local,
        mesh=mesh,
        in_specs=placed,
        out_specs=(P(("rep", "feat"), None), P("feat", None), P("feat", None)),
        check_vma=False,
    )
```

time: 82.3 us -> 65.5 us (0.80)
  Pallas kernels: 75.8 us -> 56.9 us
  local copies, waits for them, and re-layouts: 5.5 us -> 7.5 us
    pallas_call x2 -> x1, Pallas kernels: 75.8 us -> 56.9 us  [local(): pl.pallas_call(sage_kernel, out_shape=(jax.ShapeDtypeStruct((OWN, H), BF1...]
    unnamed x15 -> x17, local copies, waits for them, and re-layouts: 5.45 us -> 7.5 us
where the time goes in v2:
time: 65.5 us; the launch traced here: 65.1 us
  Pallas kernels  56.9 us (87%)
  local copies, waits for them, and re-layouts  7.5 us (11%)
  between operations  0.66 us (1%)
    pallas_call x1, Pallas kernels, local(): pl.pallas_call(sage_kernel, out_shape=(jax.ShapeDtypeStruct((OWN, H), BF1...  56.9 us
    unnamed x17, local copies, waits for them, and re-layouts  7.5 us

profile of v2, /device:TPU:1, one launch (start us, length us, event | category | flops | bytes accessed | tf_op | source)
XLA Modules:
  0.0 65.1 jit_solution(13843369301156752842)
XLA Ops:
  0.6 0.0 copy-start
  0.6 1.2 %copy-done = bf16[1,12,32768]{2,1,0:T(8,128)(2,1)S(1)} copy-done((bf16[1,12,32768]{2,1,0:T(8,128)(2,1)S(1)}, bf16[1,12,32768]{2,1,0:T(8,128)(2,1)}, u32[]{:S(2)}) %copy-start) | copy-done | bytes 786456
  1.9 0.0 copy-start.1
  1.9 0.9 %copy-done.1 = s32[3072,10]{0,1:T(8,128)S(1)} copy-done((s32[3072,10]{0,1:T(8,128)S(1)}, s32[3072,10]{0,1:T(8,128)}, u32[]{:S(2)}) %copy-start.1) | copy-done | bytes 122904
  2.8 0.0 copy-start.2
  2.8 0.7 %copy-done.2 = bf16[48,256]{1,0:T(8,128)(2,1)S(1)} copy-done((bf16[48,256]{1,0:T(8,128)(2,1)S(1)}, bf16[48,256]{1,0:T(8,128)(2,1)}, u32[]{:S(2)}) %copy-start.2) | copy-done | bytes 24600
  3.5 0.0 copy-start.3
  3.5 0.7 %copy-done.3 = s32[3072]{0:T(1024)S(1)} copy-done((s32[3072]{0:T(1024)S(1)}, s32[3072]{0:T(1024)}, u32[]{:S(2)}) %copy-start.3) | copy-done | bytes 12312
  4.2 0.0 copy-start.4
  4.2 0.7 %copy-done.4 = s32[24,16]{0,1:T(8,128)S(1)} copy-done((s32[24,16]{0,1:T(8,128)S(1)}, s32[24,16]{0,1:T(8,128)}, u32[]{:S(2)}) %copy-start.4) | copy-done | bytes 1560
  4.9 0.0 copy-start.5
  4.9 0.7 %copy-done.5 = bf16[12,256]{1,0:T(8,128)(2,1)S(1)} copy-done((bf16[12,256]{1,0:T(8,128)(2,1)S(1)}, bf16[12,256]{1,0:T(8,128)(2,1)}, u32[]{:S(2)}) %copy-start.5) | copy-done | bytes 6168
  5.6 0.0 copy-start.6
  5.6 0.7 %copy-done.6 = bf16[12,256]{1,0:T(8,128)(2,1)S(1)} copy-done((bf16[12,256]{1,0:T(8,128)(2,1)S(1)}, bf16[12,256]{1,0:T(8,128)(2,1)}, u32[]{:S(2)}) %copy-start.6) | copy-done | bytes 6168
  6.3 56.9 %exchange.1 = (bf16[48,256]{1,0:T(8,128)(2,1)S(1)}, f32[12,256]{1,0:T(8,128)S(1)}, f32[12,256]{1,0:T(8,128)S(1)}) custom-call(bf16[12,32768]{1,0:T(8,128)(2,1)S(1)} %bitcast.4, s32[16,24]{1,0:T(8,128)S(1)} %bitcast.7, s32[10,3072]{1,0:T(8,128)S(1)} %bitcast.5, s32[24,1,128]{2,1,0:T(1,128)S(1)} %bitcast.6, bf16[12,256]{1,0:T(8,128)(2,1)S(1)} %copy-done.5, ...), custom_call_target="tpu_custom_call" | custom-call | tf_op jit(solution)/shard_map/exchange/pallas_call | solution.py:274
  63.2 0.6 copy.13
  63.8 0.6 copy.14
  64.5 0.6 copy.15
Async XLA Ops:
  0.6 1.2 %copy-start = (bf16[1,12,32768]{2,1,0:T(8,128)(2,1)S(1)}, bf16[1,12,32768]{2,1,0:T(8,128)(2,1)}, u32[]{:S(2)}) copy-start(bf16[1,12,32768]{2,1,0:T(8,128)(2,1)} %param.7) | copy-start | bytes 2359300
  1.9 0.9 %copy-start.1 = (s32[3072,10]{0,1:T(8,128)S(1)}, s32[3072,10]{0,1:T(8,128)}, u32[]{:S(2)}) copy-start(s32[3072,10]{0,1:T(8,128)} %param.11) | copy-start | bytes 368644
  2.8 0.7 %copy-start.2 = (bf16[48,256]{1,0:T(8,128)(2,1)S(1)}, bf16[48,256]{1,0:T(8,128)(2,1)}, u32[]{:S(2)}) copy-start(bf16[48,256]{1,0:T(8,128)(2,1)} %dh_ref.1) | copy-start | bytes 73732
  3.5 0.7 %copy-start.3 = (s32[3072]{0:T(1024)S(1)}, s32[3072]{0:T(1024)}, u32[]{:S(2)}) copy-start(s32[3072]{0:T(1024)} %param.12) | copy-start | bytes 36868
  4.2 0.7 %copy-start.4 = (s32[24,16]{0,1:T(8,128)S(1)}, s32[24,16]{0,1:T(8,128)}, u32[]{:S(2)}) copy-start(s32[24,16]{0,1:T(8,128)} %param.10) | copy-start | bytes 4612
  4.9 0.7 %copy-start.5 = (bf16[12,256]{1,0:T(8,128)(2,1)S(1)}, bf16[12,256]{1,0:T(8,128)(2,1)}, u32[]{:S(2)}) copy-start(bf16[12,256]{1,0:T(8,128)(2,1)} %ws_ref.1) | copy-start | bytes 18436
  5.6 0.7 %copy-start.6 = (bf16[12,256]{1,0:T(8,128)(2,1)S(1)}, bf16[12,256]{1,0:T(8,128)(2,1)}, u32[]{:S(2)}) copy-start(bf16[12,256]{1,0:T(8,128)(2,1)} %wn_ref.1) | copy-start | bytes 18436

commit v3 on v2

v3 whole, which is shorter than its diff:
```python
import jax
import jax.numpy as jnp
from jax import lax
from jax.experimental import pallas as pl
from jax.experimental.pallas import tpu as pltpu
from jax.sharding import PartitionSpec as P

MESH = pl.DeviceIdType.MESH
F32, BF16 = jnp.float32, jnp.bfloat16
N = 8
TILE, TB, FAN, LISTED, NS = 128, 24, 10, 16, 256
WIDTH = 12
ROWS = 2 * WIDTH
BLOCK = 80
OWN = 48
H = 256
CHUNKS = 4
SPREAD = 4


def lane_pick(values, lanes):
    return jnp.take_along_axis(values, lanes, axis=1, mode="promise_in_bounds")


def select_tree(level, bits):
    for bit in bits:
        level = [jnp.where(bit, level[i + 1], level[i]) for i in range(0, len(level), 2)]
    return level[0]


def neighbor_sums(tiles_ref, wide, slot_ref, t):
    low, high = [], []
    for k in range(LISTED):
        block = wide[tiles_ref[k, t]]
        low.append(block[:8])
        high.append(block[8:WIDTH])
    pairs = [jnp.concatenate(high[k:k + 2], axis=0) for k in range(0, LISTED, 2)]
    upper = lax.broadcasted_iota(jnp.int32, (8, TILE), 0) >= 4
    total_low = jnp.zeros((8, TILE), F32)
    total_pair = jnp.zeros((8, TILE), F32)
    targets = pl.ds(pl.multiple_of(t * TILE, TILE), TILE)
    for j in range(FAN):
        slot = jnp.broadcast_to(slot_ref[j:j + 1, targets], (8, TILE))
        lane = slot & (TILE - 1)
        bits = [(slot & (TILE << b)) != 0 for b in range(4)]
        total_low += select_tree([lane_pick(v, lane) for v in low], bits)
        picked = select_tree([lane_pick(v, lane) for v in pairs], bits[1:])
        total_pair += jnp.where(bits[0] == upper, picked, 0.0)
    return total_low, total_pair[:4] + total_pair[4:]


def gather_block(tiles_ref, wide, slot_ref, seed_ref, turned, rows, u):
    span = 3 * TILE
    seed = jnp.concatenate([seed_ref[3 * u + i] for i in range(3)], axis=1)
    hot = (lax.broadcasted_iota(jnp.int32, (NS, span), 0) == (seed >> 7)).astype(F32).astype(BF16)
    mask = lax.broadcasted_iota(jnp.int32, (TILE, span), 0) == (seed & (TILE - 1))
    for f in range(WIDTH):
        columns = jnp.dot(turned[f], hot, preferred_element_type=F32)
        row = jnp.sum(jnp.where(mask, columns, 0.0), axis=0, keepdims=True)
        for i in range(3):
            rows[ROWS * i + f:ROWS * i + f + 1] = row[:, i * TILE:(i + 1) * TILE]
    for i in range(3):
        low, high = neighbor_sums(tiles_ref, wide, slot_ref, 3 * u + i)
        rows[ROWS * i + WIDTH:ROWS * i + 16] = high * (1.0 / FAN)
        rows[ROWS * i + 16:ROWS * (i + 1)] = low * (1.0 / FAN)
    return jnp.concatenate([rows[...], jnp.zeros((BLOCK - 3 * ROWS, TILE), F32)], axis=0).astype(BF16)


def sage_kernel(
    x_hbm, tiles_hbm, slot_hbm, seed_hbm, ws_hbm, wn_hbm, dh_hbm, hid_ref, gs_ref, gn_ref,
    x_ref, tiles_ref, slot_ref, seed_ref, ws_ref, wn_ref, dh_ref, wide, turned, rows, gb,
    xb, wb, pf, ps, pr, db, qf, qs, qr, es, er,
    l_in, x_out, x_in, w_out, w_in, v_out, v_in, p_out, p_in, d_out, d_in, q_out, q_in, e_out, e_in,
):
    rep = lax.axis_index("rep")
    feat = lax.axis_index("feat")
    b, a = feat // N, feat % N
    chunk = NS * TILE // CHUNKS

    pairs = [
        (x_hbm.at[:, pl.ds(i * chunk, chunk)], x_ref.at[:, pl.ds(i * chunk, chunk)]) for i in range(CHUNKS)
    ] + [
        (tiles_hbm, tiles_ref), (slot_hbm, slot_ref), (seed_hbm, seed_ref),
        (ws_hbm, ws_ref), (wn_hbm, wn_ref), (dh_hbm, dh_ref),
    ]
    loads = [pltpu.make_async_copy(src, dst, l_in.at[i]) for i, (src, dst) in enumerate(pairs)]
    for load in loads:
        load.start()

    def ahead(place, o):
        return lax.rem(place + o, N)

    def behind(place, o):
        return lax.rem(place + N - o, N)

    def along_b(o):
        return rep, ahead(b, o) * N + a

    def along_a(o):
        return rep, b * N + ahead(a, o)

    def along_rep(o):
        return ahead(rep, o), feat

    barrier = pltpu.get_barrier_semaphore()

    def each(body):
        def step(o, _):
            body(o)
            return 0
        lax.fori_loop(1, N, step, 0)

    def greet(way):
        return lambda o: pl.semaphore_signal(barrier, inc=1, device_id=way(o), device_id_type=MESH)

    each(greet(along_b))
    each(greet(along_a))
    each(greet(along_rep))

    def copy(src, dst, out_sem, in_sem, o, target):
        return pltpu.make_async_remote_copy(
            src_ref=src, dst_ref=dst, send_sem=out_sem.at[o], recv_sem=in_sem.at[o],
            device_id=target, device_id_type=MESH,
        )

    def x_copy(o, slot):
        return copy(gb.at[ahead(b, o)], xb.at[slot], x_out, x_in, o, along_b(o))

    def w_copy(o, slot):
        return copy(wb.at[b], wb.at[slot], w_out, w_in, o, along_b(o))

    def v_copy(o, slot):
        return copy(wb.at[rep], wb.at[slot], v_out, v_in, o, along_rep(o))

    def p_copy(o, slot):
        return copy(ps.at[ahead(a, o)], pr.at[slot], p_out, p_in, o, along_a(o))

    def d_copy(o, slot):
        return copy(db.at[a], db.at[slot], d_out, d_in, o, along_a(o))

    def q_copy(o, slot):
        return copy(qs.at[ahead(b, o)], qr.at[slot], q_out, q_in, o, along_b(o))

    def e_copy(o, slot):
        return copy(es, er.at[slot], e_out, e_in, o, along_rep(o))

    def fill(k, _):
        wide[k, :WIDTH] = x_ref[:, pl.ds(pl.multiple_of(k * TILE, TILE), TILE)].astype(F32)
        return 0

    for i in range(CHUNKS):
        loads[i].wait()
        lax.fori_loop(i * NS // CHUNKS, (i + 1) * NS // CHUNKS, fill, 0, unroll=8)
    for f in range(WIDTH):
        turned[f] = wide[:, f].T.astype(BF16)
    for load in loads[CHUNKS:]:
        load.wait()

    pl.semaphore_wait(barrier, 3 * (N - 1))

    @pl.when(b == rep)
    def _():
        mean_weight = wn_ref[...].astype(F32)
        weights = jnp.concatenate([ws_ref[...].astype(F32), mean_weight[8:], mean_weight[:8]], axis=0)
        wb[b] = jnp.concatenate([weights[:, :TILE], weights[:, TILE:]], axis=0).astype(BF16)
        each(lambda o: w_copy(o, b).start())

    def one_block(i, _):
        odd = i % 2
        away = odd * (4 - (i + 1) // 2) + (1 - odd) * (4 + i // 2)
        u = (b + away) % N
        gb[u] = gather_block(tiles_ref, wide, slot_ref, seed_ref, turned, rows, u)
        o = (u + N - b) % N

        @pl.when(o != 0)
        def _():
            x_copy(o, b).start()

        @pl.when(i == SPREAD)
        def _():
            @pl.when(b != rep)
            def _():
                w_copy((b + N - rep) % N, rep).wait_recv()

            each(lambda o: v_copy(o, rep).start())

        return 0

    lax.fori_loop(0, N, one_block, 0)
    xb[b] = gb[b]

    each(lambda o: v_copy(o, behind(rep, o)).wait_recv())
    w = wb[...].astype(F32)
    w = jnp.concatenate([w[:, :ROWS], w[:, ROWS:]], axis=2).reshape(N * ROWS, H).astype(BF16)
    each(lambda o: x_copy(o, behind(b, o)).wait_recv())
    x = xb[...].astype(F32)
    x = jnp.concatenate([x[:, ROWS * i:ROWS * (i + 1)] for i in range(3)], axis=2)
    x = x.reshape(N * ROWS, 3 * TILE).astype(BF16)
    part = lax.dot_general(x, w, (((0,), (0,)), ((), ())), preferred_element_type=F32)
    part = part.reshape(N, OWN, H)
    pf[...] = part
    ps[...] = part.astype(BF16)
    each(lambda o: p_copy(o, a).start())
    pr[a] = jnp.zeros((OWN, H), BF16)
    each(lambda o: p_copy(o, behind(a, o)).wait_recv())
    pre = pf[a] + jnp.sum(pr[...].astype(F32), axis=0)

    sigma = jax.nn.sigmoid(pre)
    db[a] = (dh_ref[...].astype(F32) * sigma * (1.0 + pre * (1.0 - sigma))).astype(BF16)
    each(lambda o: d_copy(o, a).start())
    hid_ref[...] = (pre * sigma).astype(BF16)
    each(lambda o: d_copy(o, behind(a, o)).wait_recv())

    d_pre = db[...].reshape(N * OWN, H)
    grad = jnp.dot(x, d_pre, preferred_element_type=F32).reshape(N, ROWS, H)
    grad = jnp.concatenate([grad[:, :, :TILE], grad[:, :, TILE:]], axis=1)
    qf[...] = grad
    qs[...] = grad.astype(BF16)
    each(lambda o: q_copy(o, b).start())
    qr[b] = jnp.zeros((2 * ROWS, TILE), BF16)
    each(lambda o: q_copy(o, behind(b, o)).wait_recv())
    mine = qf[b] + jnp.sum(qr[...].astype(F32), axis=0)

    es[...] = mine.astype(BF16)
    each(lambda o: e_copy(o, rep).start())
    er[rep] = mine.astype(BF16)
    each(lambda o: e_copy(o, behind(rep, o)).wait_recv())
    total = jnp.sum(er[...].astype(F32), axis=0)
    total = jnp.concatenate([total[:ROWS], total[ROWS:]], axis=1)
    gs_ref[...] = total[:WIDTH]
    gn_ref[:8] = total[16:]
    gn_ref[8:] = total[WIDTH:16]

    @pl.when(b == rep)
    def _():
        each(lambda o: w_copy(o, b).wait_send())

    each(lambda o: v_copy(o, rep).wait_send())
    each(lambda o: x_copy(o, b).wait_send())
    each(lambda o: p_copy(o, a).wait_send())
    each(lambda o: d_copy(o, a).wait_send())
    each(lambda o: q_copy(o, b).wait_send())
    each(lambda o: e_copy(o, rep).wait_send())


def local(features, w_self, w_neighbor, tile_list, nbr_slot, seed_ids, d_hidden):
    vmem = pl.BlockSpec(memory_space=pltpu.VMEM)
    dma = pltpu.SemaphoreType.DMA
    return pl.pallas_call(
        sage_kernel,
        out_shape=(
            jax.ShapeDtypeStruct((OWN, H), BF16),
            jax.ShapeDtypeStruct((WIDTH, H), F32),
            jax.ShapeDtypeStruct((WIDTH, H), F32),
        ),
        in_specs=[pl.BlockSpec(memory_space=pltpu.HBM)] * 7,
        out_specs=(vmem,) * 3,
        scratch_shapes=[
            pltpu.VMEM((WIDTH, NS * TILE), BF16),
            pltpu.SMEM((LISTED, TB), jnp.int32),
            pltpu.VMEM((FAN, TB * TILE), jnp.int32),
            pltpu.VMEM((TB, 1, TILE), jnp.int32),
            pltpu.VMEM((WIDTH, H), BF16),
            pltpu.VMEM((WIDTH, H), BF16),
            pltpu.VMEM((OWN, H), BF16),
            pltpu.VMEM((NS, 16, TILE), F32),
            pltpu.VMEM((WIDTH, TILE, NS), BF16),
            pltpu.VMEM((3 * ROWS, TILE), F32),
            pltpu.VMEM((N, BLOCK, TILE), BF16),
            pltpu.VMEM((N, BLOCK, TILE), BF16),
            pltpu.VMEM((N, 2 * ROWS, TILE), BF16),
            pltpu.VMEM((N, OWN, H), F32),
            pltpu.VMEM((N, OWN, H), BF16),
            pltpu.VMEM((N, OWN, H), BF16),
            pltpu.VMEM((N, OWN, H), BF16),
            pltpu.VMEM((N, 2 * ROWS, TILE), F32),
            pltpu.VMEM((N, 2 * ROWS, TILE), BF16),
            pltpu.VMEM((N, 2 * ROWS, TILE), BF16),
            pltpu.VMEM((2 * ROWS, TILE), BF16),
            pltpu.VMEM((N, 2 * ROWS, TILE), BF16),
        ]
        + [dma((CHUNKS + 6,))] + [dma((N,))] * 14,
        compiler_params=pltpu.CompilerParams(
            collective_id=0, has_side_effects=True, vmem_limit_bytes=63 * 2**20
        ),
        name="exchange",
    )(
        features[0], tile_list.T, nbr_slot.T, seed_ids.reshape(TB, 1, TILE), w_self, w_neighbor, d_hidden
    )


def solution(mesh):
    placed = (
        P("rep", "feat", None),
        P("feat", None),
        P("feat", None),
        P("rep", None),
        P("rep", None),
        P("rep"),
        P(("rep", "feat"), None),
    )
    return jax.shard_map(
        local,
        mesh=mesh,
        in_specs=placed,
        out_specs=(P(("rep", "feat"), None), P("feat", None), P("feat", None)),
        check_vma=False,
    )
```

time: 65.5 us -> 59.8 us (0.913)
  local copies, waits for them, and re-layouts: 7.5 us -> 2.69 us
  Pallas kernels: 56.9 us -> 56.2 us
    unnamed x17 -> x7, local copies, waits for them, and re-layouts: 7.5 us -> 2.69 us
    pallas_call x1, Pallas kernels: 56.9 us -> 56.2 us  [local(): pl.pallas_call(sage_kernel, out_shape=(jax.ShapeDtypeStruct((OWN, H), BF1...]
where the time goes in v3:
time: 59.8 us; the launch traced here: 59.5 us
  Pallas kernels  56.2 us (94%)
  local copies, waits for them, and re-layouts  2.69 us (4%)
  between operations  0.65 us (1%)
    pallas_call x1, Pallas kernels, local(): pl.pallas_call(sage_kernel, out_shape=(jax.ShapeDtypeStruct((OWN, H), BF1...  56.2 us
    unnamed x7, local copies, waits for them, and re-layouts  2.69 us

profile of v3, /device:TPU:1, one launch (start us, length us, event | category | flops | bytes accessed | tf_op | source)
XLA Modules:
  0.0 59.5 jit_solution(16733138920668637502)
XLA Ops:
  0.6 56.2 %exchange.1 = (bf16[48,256]{1,0:T(8,128)(2,1)}, f32[12,256]{1,0:T(8,128)}, f32[12,256]{1,0:T(8,128)}) custom-call(bf16[12,32768]{1,0:T(8,128)(2,1)} %bitcast.4, s32[16,24]{1,0:T(8,128)} %bitcast.7, s32[10,3072]{1,0:T(8,128)} %bitcast.5, s32[24,1,128]{2,1,0:T(1,128)} %bitcast.6, bf16[12,256]{1,0:T(8,128)(2,1)} %ws_hbm.1, bf16[12,256]{1,0:T(8,128)(2,1)} %wn_hbm.1, ...), custom_call_target="tpu_custom_call" | custom-call | tf_op jit(solution)/shard_map/exchange/pallas_call | solution.py:249
  56.8 0.0 copy-start.1
  56.9 1.4 %copy.13 = bf16[48,256]{1,0:T(8,128)(2,1)} copy(bf16[48,256]{1,0:T(8,128)(2,1)} %get-tuple-element.6) | data formatting | bytes 49152
  58.2 0.0 copy-done.1
  58.2 0.0 copy-start
  58.2 0.6 %copy.14 = f32[12,256]{1,0:T(8,128)} copy(f32[12,256]{1,0:T(8,128)S(1)} %copy-done.1) | data formatting | bytes 24576
  58.8 0.1 copy-done
  58.9 0.6 %copy.15 = f32[12,256]{1,0:T(8,128)} copy(f32[12,256]{1,0:T(8,128)S(1)} %copy-done) | data formatting | bytes 24576
Async XLA Ops:
  56.8 1.4 %copy-start.1 = (f32[12,256]{1,0:T(8,128)S(1)}, f32[12,256]{1,0:T(8,128)}, u32[]{:S(2)}) copy-start(f32[12,256]{1,0:T(8,128)} %get-tuple-element.7) | copy-start | bytes 36868
  58.2 0.7 %copy-start = (f32[12,256]{1,0:T(8,128)S(1)}, f32[12,256]{1,0:T(8,128)}, u32[]{:S(2)}) copy-start(f32[12,256]{1,0:T(8,128)} %get-tuple-element.8) | copy-start | bytes 36868

commit v4 on v3

--- a/solution.py
+++ b/solution.py
@@ -15,7 +15,7 @@
 OWN = 48
 H = 256
 CHUNKS = 4
-SPREAD = 4
+AHEAD = 4
 
 
 def lane_pick(values, lanes):
@@ -156,39 +156,48 @@
     for load in loads[CHUNKS:]:
         load.wait()
 
-    pl.semaphore_wait(barrier, 3 * (N - 1))
-
     @pl.when(b == rep)
     def _():
         mean_weight = wn_ref[...].astype(F32)
         weights = jnp.concatenate([ws_ref[...].astype(F32), mean_weight[8:], mean_weight[:8]], axis=0)
         wb[b] = jnp.concatenate([weights[:, :TILE], weights[:, TILE:]], axis=0).astype(BF16)
-        each(lambda o: w_copy(o, b).start())
-
-    def one_block(i, _):
+
+    def block_at(i):
         odd = i % 2
         away = odd * (4 - (i + 1) // 2) + (1 - odd) * (4 + i // 2)
-        u = (b + away) % N
+        return (b + away) % N
+
+    def send_block(i):
+        x_copy((block_at(i) + N - b) % N, b).start()
+
+    def one_block(i, _):
+        u = block_at(i)
         gb[u] = gather_block(tiles_ref, wide, slot_ref, seed_ref, turned, rows, u)
-        o = (u + N - b) % N
-
-        @pl.when(o != 0)
+
+        @pl.when(i == AHEAD - 1)
         def _():
-            x_copy(o, b).start()
-
-        @pl.when(i == SPREAD)
+            pl.semaphore_wait(barrier, 3 * (N - 1))
+
+            @pl.when(b == rep)
+            def _():
+                each(lambda o: w_copy(o, b).start())
+
+            lax.fori_loop(0, AHEAD - 1, lambda k, _: (send_block(k), 0)[1], 0)
+
+        @pl.when((i >= AHEAD - 1) & (i < N - 1))
         def _():
-            @pl.when(b != rep)
-            def _():
-                w_copy((b + N - rep) % N, rep).wait_recv()
-
-            each(lambda o: v_copy(o, rep).start())
+            send_block(i)
 
         return 0
 
     lax.fori_loop(0, N, one_block, 0)
     xb[b] = gb[b]
 
+    @pl.when(b != rep)
+    def _():
+        w_copy((b + N - rep) % N, rep).wait_recv()
+
+    each(lambda o: v_copy(o, rep).start())
     each(lambda o: v_copy(o, behind(rep, o)).wait_recv())
     w = wb[...].astype(F32)
     w = jnp.concatenate([w[:, :ROWS], w[:, ROWS:]], axis=2).reshape(N * ROWS, H).astype(BF16)
@@ -243,10 +252,16 @@
     each(lambda o: e_copy(o, rep).wait_send())
 
 
+def write_kernel(hid_in, gs_in, gn_in, hid_out, gs_out, gn_out):
+    hid_out[...] = hid_in[...]
+    gs_out[...] = gs_in[...]
+    gn_out[...] = gn_in[...]
+
+
 def local(features, w_self, w_neighbor, tile_list, nbr_slot, seed_ids, d_hidden):
     vmem = pl.BlockSpec(memory_space=pltpu.VMEM)
     dma = pltpu.SemaphoreType.DMA
-    return pl.pallas_call(
+    results = pl.pallas_call(
         sage_kernel,
         out_shape=(
             jax.ShapeDtypeStruct((OWN, H), BF16),
@@ -287,6 +302,13 @@
     )(
         features[0], tile_list.T, nbr_slot.T, seed_ids.reshape(TB, 1, TILE), w_self, w_neighbor, d_hidden
     )
+    return pl.pallas_call(
+        write_kernel,
+        out_shape=tuple(jax.ShapeDtypeStruct(r.shape, r.dtype) for r in results),
+        in_specs=[vmem] * 3,
+        out_specs=(vmem,) * 3,
+        name="write",
+    )(*results)
 
 
 def solution(mesh):

time: 59.8 us -> 55.8 us (0.933)
  local copies, waits for them, and re-layouts: 2.69 us -> 0 us
  Pallas kernels: 56.2 us -> 54.9 us
    unnamed x7 -> x0, local copies, waits for them, and re-layouts: 2.69 us -> none
    pallas_call x1, Pallas kernels: 56.2 us -> 53.6 us  [local(): pl.pallas_call(sage_kernel, out_shape=(jax.ShapeDtypeStruct((OWN, H), BF1...]
    pallas_call x0 -> x1, Pallas kernels: none -> 1.38 us  [local(): pl.pallas_call(write_kernel, out_shape=tuple((jax.ShapeDtypeStruct(r.shap...]
where the time goes in v4:
time: 55.8 us; the launch traced here: 55.6 us
  Pallas kernels  54.9 us (98%)
  between operations  0.64 us (1%)
    pallas_call x1, Pallas kernels, local(): pl.pallas_call(sage_kernel, out_shape=(jax.ShapeDtypeStruct((OWN, H), BF1...  53.6 us
    pallas_call x1, Pallas kernels, local(): pl.pallas_call(write_kernel, out_shape=tuple((jax.ShapeDtypeStruct(r.shap...  1.38 us

profile of v4, /device:TPU:1, one launch (start us, length us, event | category | flops | bytes accessed | tf_op | source)
XLA Modules:
  0.0 55.6 jit_solution(10458531204199216779)
XLA Ops:
  0.6 53.6 %exchange.1 = (bf16[48,256]{1,0:T(8,128)(2,1)}, f32[12,256]{1,0:T(8,128)}, f32[12,256]{1,0:T(8,128)}) custom-call(bf16[12,32768]{1,0:T(8,128)(2,1)} %bitcast.4, s32[16,24]{1,0:T(8,128)} %bitcast.7, s32[10,3072]{1,0:T(8,128)} %bitcast.5, s32[24,1,128]{2,1,0:T(1,128)} %bitcast.6, bf16[12,256]{1,0:T(8,128)(2,1)} %ws_hbm.1, bf16[12,256]{1,0:T(8,128)(2,1)} %wn_hbm.1, ...), custom_call_target="tpu_custom_call" | custom-call | tf_op jit(solution)/shard_map/exchange/pallas_call | solution.py:264
  54.2 1.4 %write.1 = (bf16[48,256]{1,0:T(8,128)(2,1)}, f32[12,256]{1,0:T(8,128)}, f32[12,256]{1,0:T(8,128)}) custom-call(bf16[48,256]{1,0:T(8,128)(2,1)} %get-tuple-element.6.hid_in, f32[12,256]{1,0:T(8,128)} %get-tuple-element.7.gs_in, f32[12,256]{1,0:T(8,128)} %get-tuple-element.8.gn_in), custom_call_target="tpu_custom_call" | custom-call | tf_op jit(solution)/shard_map/write/pallas_call | solution.py:305

commit v5 on v4

--- a/solution.py
+++ b/solution.py
@@ -104,11 +104,9 @@
 
     barrier = pltpu.get_barrier_semaphore()
 
-    def each(body):
-        def step(o, _):
+    def each(body, order=(4, 3, 5, 2, 6, 1, 7)):
+        for o in order:
             body(o)
-            return 0
-        lax.fori_loop(1, N, step, 0)
 
     def greet(way):
         return lambda o: pl.semaphore_signal(barrier, inc=1, device_id=way(o), device_id_type=MESH)
@@ -209,14 +207,14 @@
     part = part.reshape(N, OWN, H)
     pf[...] = part
     ps[...] = part.astype(BF16)
-    each(lambda o: p_copy(o, a).start())
+    each(lambda o: p_copy(o, a).start(), (2, 6, 1, 3, 5, 7, 4))
     pr[a] = jnp.zeros((OWN, H), BF16)
     each(lambda o: p_copy(o, behind(a, o)).wait_recv())
     pre = pf[a] + jnp.sum(pr[...].astype(F32), axis=0)
 
     sigma = jax.nn.sigmoid(pre)
     db[a] = (dh_ref[...].astype(F32) * sigma * (1.0 + pre * (1.0 - sigma))).astype(BF16)
-    each(lambda o: d_copy(o, a).start())
+    each(lambda o: d_copy(o, a).start(), (2, 6, 1, 3, 5, 7, 4))
     hid_ref[...] = (pre * sigma).astype(BF16)
     each(lambda o: d_copy(o, behind(a, o)).wait_recv())
 

time: 55.8 us -> 54.2 us (0.971)
  Pallas kernels: 54.9 us -> 53.4 us
    pallas_call x1, Pallas kernels: 53.6 us -> 52 us  [local(): pl.pallas_call(sage_kernel, out_shape=(jax.ShapeDtypeStruct((OWN, H), BF1...]
where the time goes in v5:
time: 54.2 us; the launch traced here: 54 us
  Pallas kernels  53.4 us (99%)
  between operations  0.64 us (1%)
    pallas_call x1, Pallas kernels, local(): pl.pallas_call(sage_kernel, out_shape=(jax.ShapeDtypeStruct((OWN, H), BF1...  52 us
    pallas_call x1, Pallas kernels, local(): pl.pallas_call(write_kernel, out_shape=tuple((jax.ShapeDtypeStruct(r.shap...  1.38 us

profile of v5, /device:TPU:1, one launch (start us, length us, event | category | flops | bytes accessed | tf_op | source)
XLA Modules:
  0.0 54.0 jit_solution(2294161563749636744)
XLA Ops:
  0.6 52.0 %exchange.1 = (bf16[48,256]{1,0:T(8,128)(2,1)}, f32[12,256]{1,0:T(8,128)}, f32[12,256]{1,0:T(8,128)}) custom-call(bf16[12,32768]{1,0:T(8,128)(2,1)} %bitcast.4, s32[16,24]{1,0:T(8,128)} %bitcast.7, s32[10,3072]{1,0:T(8,128)} %bitcast.5, s32[24,1,128]{2,1,0:T(1,128)} %bitcast.6, bf16[12,256]{1,0:T(8,128)(2,1)} %ws_hbm.1, bf16[12,256]{1,0:T(8,128)(2,1)} %wn_hbm.1, ...), custom_call_target="tpu_custom_call" | custom-call | tf_op jit(solution)/shard_map/exchange/pallas_call | solution.py:262
  52.7 1.4 %write.1 = (bf16[48,256]{1,0:T(8,128)(2,1)}, f32[12,256]{1,0:T(8,128)}, f32[12,256]{1,0:T(8,128)}) custom-call(bf16[48,256]{1,0:T(8,128)(2,1)} %get-tuple-element.6.hid_in, f32[12,256]{1,0:T(8,128)} %get-tuple-element.7.gs_in, f32[12,256]{1,0:T(8,128)} %get-tuple-element.8.gn_in), custom_call_target="tpu_custom_call" | custom-call | tf_op jit(solution)/shard_map/write/pallas_call | solution.py:303

commit v6 on v5

--- a/solution.py
+++ b/solution.py
@@ -84,9 +84,6 @@
         (ws_hbm, ws_ref), (wn_hbm, wn_ref), (dh_hbm, dh_ref),
     ]
     loads = [pltpu.make_async_copy(src, dst, l_in.at[i]) for i, (src, dst) in enumerate(pairs)]
-    for load in loads:
-        load.start()
-
     def ahead(place, o):
         return lax.rem(place + o, N)
 
@@ -114,6 +111,9 @@
     each(greet(along_b))
     each(greet(along_a))
     each(greet(along_rep))
+
+    for load in loads:
+        load.start()
 
     def copy(src, dst, out_sem, in_sem, o, target):
         return pltpu.make_async_remote_copy(
@@ -180,7 +180,8 @@
             def _():
                 each(lambda o: w_copy(o, b).start())
 
-            lax.fori_loop(0, AHEAD - 1, lambda k, _: (send_block(k), 0)[1], 0)
+            for k in range(AHEAD - 1):
+                send_block(k)
 
         @pl.when((i >= AHEAD - 1) & (i < N - 1))
         def _():
@@ -250,10 +251,17 @@
     each(lambda o: e_copy(o, rep).wait_send())
 
 
-def write_kernel(hid_in, gs_in, gn_in, hid_out, gs_out, gn_out):
-    hid_out[...] = hid_in[...]
-    gs_out[...] = gs_in[...]
-    gn_out[...] = gn_in[...]
+def write_kernel(hid_in, gs_in, gn_in, hid_out, gs_out, gn_out, hid, gs, gn, sems):
+    moves = [(hid_in, hid, hid_out), (gs_in, gs, gs_out), (gn_in, gn, gn_out)]
+    reads = [pltpu.make_async_copy(src, mid, sems.at[i]) for i, (src, mid, _) in enumerate(moves)]
+    writes = [pltpu.make_async_copy(mid, dst, sems.at[3 + i]) for i, (_, mid, dst) in enumerate(moves)]
+    for read in reads:
+        read.start()
+    for read, write in zip(reads, writes):
+        read.wait()
+        write.start()
+    for write in writes:
+        write.wait()
 
 
 def local(features, w_self, w_neighbor, tile_list, nbr_slot, seed_ids, d_hidden):
@@ -303,8 +311,10 @@
     return pl.pallas_call(
         write_kernel,
         out_shape=tuple(jax.ShapeDtypeStruct(r.shape, r.dtype) for r in results),
-        in_specs=[vmem] * 3,
-        out_specs=(vmem,) * 3,
+        in_specs=[pl.BlockSpec(memory_space=pl.ANY)] * 3,
+        out_specs=(pl.BlockSpec(memory_space=pl.ANY),) * 3,
+        scratch_shapes=[pltpu.VMEM(r.shape, r.dtype) for r in results] + [dma((6,))],
+        compiler_params=pltpu.CompilerParams(vmem_limit_bytes=63 * 2**20),
         name="write",
     )(*results)
 

time: 54.2 us -> 54.4 us (level)
  no operation moved by 1% of the time
where the time goes in v6:
time: 54.4 us; the launch traced here: 54.2 us
  Pallas kernels  53.5 us (98%)
  between operations  0.64 us (1%)
    pallas_call x1, Pallas kernels, local(): pl.pallas_call(sage_kernel, out_shape=(jax.ShapeDtypeStruct((OWN, H), BF1...  52.1 us
    pallas_call x1, Pallas kernels, local(): pl.pallas_call(write_kernel, out_shape=tuple((jax.ShapeDtypeStruct(r.shap...  1.41 us

profile of v6, /device:TPU:1, one launch (start us, length us, event | category | flops | bytes accessed | tf_op | source)
XLA Modules:
  0.0 54.2 jit_solution(4708194791633231631)
XLA Ops:
  0.6 52.1 %exchange.1 = (bf16[48,256]{1,0:T(8,128)(2,1)}, f32[12,256]{1,0:T(8,128)}, f32[12,256]{1,0:T(8,128)}) custom-call(bf16[12,32768]{1,0:T(8,128)(2,1)} %bitcast.4, s32[16,24]{1,0:T(8,128)} %bitcast.7, s32[10,3072]{1,0:T(8,128)} %bitcast.5, s32[24,1,128]{2,1,0:T(1,128)} %bitcast.6, bf16[12,256]{1,0:T(8,128)(2,1)} %ws_hbm.1, bf16[12,256]{1,0:T(8,128)(2,1)} %wn_hbm.1, ...), custom_call_target="tpu_custom_call" | custom-call | tf_op jit(solution)/shard_map/exchange/pallas_call | solution.py:270
  52.8 1.4 %write.1 = (bf16[48,256]{1,0:T(8,128)(2,1)}, f32[12,256]{1,0:T(8,128)}, f32[12,256]{1,0:T(8,128)}) custom-call(bf16[48,256]{1,0:T(8,128)(2,1)} %get-tuple-element.6.hid_in, f32[12,256]{1,0:T(8,128)} %get-tuple-element.7.gs_in, f32[12,256]{1,0:T(8,128)} %get-tuple-element.8.gn_in), custom_call_target="tpu_custom_call" | custom-call | tf_op jit(solution)/shard_map/write/pallas_call | solution.py:311

commit v7 on v6

--- a/solution.py
+++ b/solution.py
@@ -232,6 +232,14 @@
     es[...] = mine.astype(BF16)
     each(lambda o: e_copy(o, rep).start())
     er[rep] = mine.astype(BF16)
+    @pl.when(b == rep)
+    def _():
+        each(lambda o: w_copy(o, b).wait_send())
+
+    each(lambda o: v_copy(o, rep).wait_send())
+    each(lambda o: x_copy(o, b).wait_send())
+    each(lambda o: p_copy(o, a).wait_send())
+    each(lambda o: d_copy(o, a).wait_send())
     each(lambda o: e_copy(o, behind(rep, o)).wait_recv())
     total = jnp.sum(er[...].astype(F32), axis=0)
     total = jnp.concatenate([total[:ROWS], total[ROWS:]], axis=1)
@@ -239,14 +247,6 @@
     gn_ref[:8] = total[16:]
     gn_ref[8:] = total[WIDTH:16]
 
-    @pl.when(b == rep)
-    def _():
-        each(lambda o: w_copy(o, b).wait_send())
-
-    each(lambda o: v_copy(o, rep).wait_send())
-    each(lambda o: x_copy(o, b).wait_send())
-    each(lambda o: p_copy(o, a).wait_send())
-    each(lambda o: d_copy(o, a).wait_send())
     each(lambda o: q_copy(o, b).wait_send())
     each(lambda o: e_copy(o, rep).wait_send())
 

time: 54.4 us -> 54.3 us (level)
  no operation moved by 1% of the time
where the time goes in v7:
time: 54.3 us; the launch traced here: 54.1 us
  Pallas kernels  53.5 us (99%)
  between operations  0.64 us (1%)
    pallas_call x1, Pallas kernels, local(): pl.pallas_call(sage_kernel, out_shape=(jax.ShapeDtypeStruct((OWN, H), BF1...  52.1 us
    pallas_call x1, Pallas kernels, local(): pl.pallas_call(write_kernel, out_shape=tuple((jax.ShapeDtypeStruct(r.shap...  1.41 us

profile of v7, /device:TPU:1, one launch (start us, length us, event | category | flops | bytes accessed | tf_op | source)
XLA Modules:
  0.0 54.1 jit_solution(13536665237263501083)
XLA Ops:
  0.6 52.1 %exchange.1 = (bf16[48,256]{1,0:T(8,128)(2,1)}, f32[12,256]{1,0:T(8,128)}, f32[12,256]{1,0:T(8,128)}) custom-call(bf16[12,32768]{1,0:T(8,128)(2,1)} %bitcast.4, s32[16,24]{1,0:T(8,128)} %bitcast.7, s32[10,3072]{1,0:T(8,128)} %bitcast.5, s32[24,1,128]{2,1,0:T(1,128)} %bitcast.6, bf16[12,256]{1,0:T(8,128)(2,1)} %ws_hbm.1, bf16[12,256]{1,0:T(8,128)(2,1)} %wn_hbm.1, ...), custom_call_target="tpu_custom_call" | custom-call | tf_op jit(solution)/shard_map/exchange/pallas_call | solution.py:270
  52.7 1.4 %write.1 = (bf16[48,256]{1,0:T(8,128)(2,1)}, f32[12,256]{1,0:T(8,128)}, f32[12,256]{1,0:T(8,128)}) custom-call(bf16[48,256]{1,0:T(8,128)(2,1)} %get-tuple-element.6.hid_in, f32[12,256]{1,0:T(8,128)} %get-tuple-element.7.gs_in, f32[12,256]{1,0:T(8,128)} %get-tuple-element.8.gn_in), custom_call_target="tpu_custom_call" | custom-call | tf_op jit(solution)/shard_map/write/pallas_call | solution.py:311
